TPU v7x, 512 devices: a whole 4x8x8 slice. The times are simulated.
512 devices in a mesh: cmp: 32 (over z, x), tgt: 16 (over y, core).
Axes of the slice: x: 4, y: 8, z: 8, core: 2. Of those that a mesh axis runs over, the one named last changes fastest.
Arguments:
- responses: bfloat16 [8192, 1024, 128], P('cmp', 'tgt'), may hold values from -33 to 33
- target_init: bfloat16 [1024, 64], P('tgt'), may hold values from -5 to 5
- condition_factor: bfloat16 [128, 64], replicated, may hold values from -0.5 to 0.5
Outputs:
- compound_factor: float32 [8192, 64], P('cmp')
- target_factor: float32 [1024, 64], P('tgt')
All inputs are finite; a program needn't handle non-finite values.
Results may differ from a plain program's by a relative error of at most 0.0003.
Values sent between devices are 32-bit elements; how exact they have to be, the bound alone decides.
A program may use at most 64 MiB of HBM per device.

v0:
```python
import jax
import jax.numpy as jnp
from jax import lax
from jax.sharding import PartitionSpec as P

ITERS = 5


def gram_of(factor):
    return jnp.dot(
        factor.T, factor, precision=lax.Precision.HIGHEST, preferred_element_type=jnp.float32
    )


def solve_normal(rhs, normal):
    lower = jnp.linalg.cholesky(normal)
    middle = lax.linalg.triangular_solve(lower, rhs, left_side=False, lower=True, transpose_a=True)
    return lax.linalg.triangular_solve(
        lower, middle, left_side=False, lower=True, transpose_a=False
    )


def target_total(partial_gram):
    return lax.psum(partial_gram, "tgt")


def body(responses, target_init, condition_factor):
    cmp_rows = responses.shape[0]
    tgt_rows = responses.shape[1]
    cond_count = responses.shape[2]
    rank_width = condition_factor.shape[1]
    cond = condition_factor.astype(jnp.float32)
    cond_gram = gram_of(cond)
    flat = jnp.dot(
        responses.reshape(cmp_rows * tgt_rows, cond_count),
        condition_factor,
        preferred_element_type=jnp.float32,
    )
    shared = flat.reshape(cmp_rows, tgt_rows, rank_width)

    def fetch():
        return shared

    target_raw = target_init.astype(jnp.float32)
    pending = gram_of(target_raw)
    target_gram = target_total(pending)
    compound_raw = jnp.zeros((cmp_rows, rank_width), jnp.float32)
    compound_gram = jnp.zeros((rank_width, rank_width), jnp.float32)
    for sweep in range(ITERS):
        inner = fetch()
        first = jnp.einsum("ijr,jr->ir", inner, target_raw, precision=lax.Precision.HIGHEST)
        summed = lax.psum(first, "tgt")
        compound_raw = solve_normal(summed, target_gram * cond_gram)
        inner_again = fetch()
        second = jnp.einsum(
            "ijr,ir->jr", inner_again, compound_raw, precision=lax.Precision.HIGHEST
        )
        target_sum, compound_gram = lax.psum((second, gram_of(compound_raw)), "cmp")
        target_raw = solve_normal(target_sum, compound_gram * cond_gram)
        pending = gram_of(target_raw)
        target_gram = target_total(pending)
    compound_count = cmp_rows * lax.axis_size("cmp")
    target_count = tgt_rows * lax.axis_size("tgt")
    compound_factor = (
        compound_raw / jnp.sqrt(jnp.diagonal(compound_gram) / compound_count + 1e-06)[None, :]
    )
    target_factor = target_raw / jnp.sqrt(jnp.diagonal(target_gram) / target_count + 1e-06)[None, :]
    return (compound_factor, target_factor)


def solution(mesh):
    return jax.shard_map(
        body,
        mesh=mesh,
        in_specs=(P("cmp", "tgt", None), P("tgt", None), P()),
        out_specs=(P("cmp", None), P("tgt", None)),
        check_vma=False,
    )
```

profile of v0, /device:TPU:1, one launch (start us, length us, event | category | flops | bytes accessed | tf_op | source)
XLA Modules:
  0.0 1432.0 jit_solution(13418670611447832796)
XLA Ops:
  8.1 6.6 fusion
  14.7 1.9 copy-done.1
  16.6 3.8 fusion.20
  21.3 49.4 %psum.147 = f32[64,64]{0,1:T(8,128)S(1)} all-reduce(f32[64,64]{0,1:T(8,128)S(1)} %fusion.112), channel_id=1, replica_groups=mesh['cmp'=32,'tgt'=16] {'tgt'}, use_global_device_ids=true, to_apply=%region_0.0 | all-reduce | flops 4096 | bytes 32768 | tf_op jit(solution)/shard_map/psum | solution.py:24
  70.9 5.8 cholesky.164
  78.1 4.9 custom-call.35
  83.0 48.8 %all-reduce.11.cloned.1.call-done = f32[256,64]{0,1:T(8,128)} async-done(((f32[256,64]{0,1:T(8,128)}), f32[256,64]{0,1:T(8,128)}) %all-reduce.11.cloned.1.call-update) | async-done | bytes 65552 | tf_op jit(solution)/shard_map/psum | solution.py:52
  133.3 7.7 fusion.18
  141.0 116.7 %all-reduce.4 = (f32[64,64]{0,1:T(8,128)S(1)}, f32[64,64]{0,1:T(8,128)S(1)}) all-reduce(f32[64,64]{0,1:T(8,128)S(1)} %bitcast.303, f32[64,64]{0,1:T(8,128)S(1)} %fusion.30), channel_id=1, replica_groups=mesh['cmp'=32,'tgt'=16] {'cmp'}, use_global_device_ids=true, to_apply=%region_5.9 | all-reduce | flops 8192 | bytes 65536 | tf_op jit(solution)/shard_map/psum | solution.py:58
  257.8 5.8 cholesky.175
  265.0 4.9 custom-call.37
  270.5 6.4 fusion.16
  277.6 70.0 %psum.151 = f32[64,64]{0,1:T(8,128)S(1)} all-reduce(f32[64,64]{0,1:T(8,128)S(1)} %fusion.84), channel_id=1, replica_groups=mesh['cmp'=32,'tgt'=16] {'tgt'}, use_global_device_ids=true, to_apply=%region_6.12 | all-reduce | flops 4096 | bytes 32768 | tf_op jit(solution)/shard_map/psum | solution.py:24
  347.8 5.8 cholesky.186
  355.0 4.9 custom-call.39
  359.9 42.7 %all-reduce.13.cloned.1.call-done = f32[256,64]{0,1:T(8,128)} async-done(((f32[256,64]{0,1:T(8,128)}), f32[256,64]{0,1:T(8,128)}) %all-reduce.13.cloned.1.call-update) | async-done | bytes 65552 | tf_op jit(solution)/shard_map/psum | solution.py:52
  404.1 7.7 fusion.14
  411.8 116.4 %all-reduce.3 = (f32[64,64]{0,1:T(8,128)S(1)}, f32[64,64]{0,1:T(8,128)S(1)}) all-reduce(f32[64,64]{0,1:T(8,128)S(1)} %bitcast.304, f32[64,64]{0,1:T(8,128)S(1)} %fusion.28), channel_id=1, replica_groups=mesh['cmp'=32,'tgt'=16] {'cmp'}, use_global_device_ids=true, to_apply=%region_9.15 | all-reduce | flops 8192 | bytes 65536 | tf_op jit(solution)/shard_map/psum | solution.py:58
  528.3 5.8 cholesky.197
  535.4 4.9 custom-call.41
  541.0 6.4 fusion.12
  548.1 70.1 %psum.155 = f32[64,64]{0,1:T(8,128)S(1)} all-reduce(f32[64,64]{0,1:T(8,128)S(1)} %fusion.74), channel_id=1, replica_groups=mesh['cmp'=32,'tgt'=16] {'tgt'}, use_global_device_ids=true, to_apply=%region_10.16 | all-reduce | flops 4096 | bytes 32768 | tf_op jit(solution)/shard_map/psum | solution.py:24
  618.3 5.8 cholesky.208
  625.5 4.9 custom-call.43
  630.4 42.7 %all-reduce.15.cloned.1.call-done = f32[256,64]{0,1:T(8,128)} async-done(((f32[256,64]{0,1:T(8,128)}), f32[256,64]{0,1:T(8,128)}) %all-reduce.15.cloned.1.call-update) | async-done | bytes 65552 | tf_op jit(solution)/shard_map/psum | solution.py:52
  674.6 7.7 fusion.10
  682.3 116.4 %all-reduce.2 = (f32[64,64]{0,1:T(8,128)S(1)}, f32[64,64]{0,1:T(8,128)S(1)}) all-reduce(f32[64,64]{0,1:T(8,128)S(1)} %bitcast.305, f32[64,64]{0,1:T(8,128)S(1)} %fusion.26), channel_id=1, replica_groups=mesh['cmp'=32,'tgt'=16] {'cmp'}, use_global_device_ids=true, to_apply=%region_13.19 | all-reduce | flops 8192 | bytes 65536 | tf_op jit(solution)/shard_map/psum | solution.py:58
  798.8 5.8 cholesky.219
  806.0 4.9 custom-call.45
  811.5 6.4 fusion.8
  818.7 70.4 %psum.159 = f32[64,64]{0,1:T(8,128)S(1)} all-reduce(f32[64,64]{0,1:T(8,128)S(1)} %fusion.64), channel_id=1, replica_groups=mesh['cmp'=32,'tgt'=16] {'tgt'}, use_global_device_ids=true, to_apply=%region_14.20 | all-reduce | flops 4096 | bytes 32768 | tf_op jit(solution)/shard_map/psum | solution.py:24
  889.2 5.8 cholesky.230
  896.4 4.9 custom-call.47
  901.3 42.4 %all-reduce.17.cloned.1.call-done = f32[256,64]{0,1:T(8,128)} async-done(((f32[256,64]{0,1:T(8,128)}), f32[256,64]{0,1:T(8,128)}) %all-reduce.17.cloned.1.call-update) | async-done | bytes 65552 | tf_op jit(solution)/shard_map/psum | solution.py:52
  945.2 7.7 fusion.6
  952.9 116.3 %all-reduce.1 = (f32[64,64]{0,1:T(8,128)S(1)}, f32[64,64]{0,1:T(8,128)S(1)}) all-reduce(f32[64,64]{0,1:T(8,128)S(1)} %bitcast.306, f32[64,64]{0,1:T(8,128)S(1)} %fusion.24), channel_id=1, replica_groups=mesh['cmp'=32,'tgt'=16] {'cmp'}, use_global_device_ids=true, to_apply=%region_17.23 | all-reduce | flops 8192 | bytes 65536 | tf_op jit(solution)/shard_map/psum | solution.py:58
  1069.3 5.8 cholesky.241
  1076.5 4.9 custom-call.49
  1082.1 6.4 fusion.4
  1089.2 70.1 %psum.163 = f32[64,64]{0,1:T(8,128)S(1)} all-reduce(f32[64,64]{0,1:T(8,128)S(1)} %fusion.54), channel_id=1, replica_groups=mesh['cmp'=32,'tgt'=16] {'tgt'}, use_global_device_ids=true, to_apply=%region_18.24 | all-reduce | flops 4096 | bytes 32768 | tf_op jit(solution)/shard_map/psum | solution.py:24
  1159.4 5.8 cholesky.252
  1166.5 4.9 custom-call.51
  1171.4 42.7 %all-reduce.19.cloned.1.call-done = f32[256,64]{0,1:T(8,128)} async-done(((f32[256,64]{0,1:T(8,128)}), f32[256,64]{0,1:T(8,128)}) %all-reduce.19.cloned.1.call-update) | async-done | bytes 65552 | tf_op jit(solution)/shard_map/psum | solution.py:52
  1215.7 7.7 fusion.2
  1223.4 116.2 %all-reduce = (f32[64,64]{0,1:T(8,128)S(1)}, f32[64,64]{0,1:T(8,128)S(1)}) all-reduce(f32[64,64]{0,1:T(8,128)S(1)} %fusion.22, f32[64,64]{0,1:T(8,128)S(1)} %bitcast.307), channel_id=1, replica_groups=mesh['cmp'=32,'tgt'=16] {'cmp'}, use_global_device_ids=true, to_apply=%region_20.26 | all-reduce | flops 8192 | bytes 65536 | tf_op jit(solution)/shard_map/psum | solution.py:58
  1341.1 5.8 cholesky.263
  1348.3 4.9 custom-call.53
  1353.8 69.8 %psum.167 = f32[64,64]{1,0:T(8,128)S(1)} all-reduce(f32[64,64]{1,0:T(8,128)S(1)} %fusion.113), channel_id=1, replica_groups=mesh['cmp'=32,'tgt'=16] {'tgt'}, use_global_device_ids=true, to_apply=%region_22.28 | all-reduce | flops 4096 | bytes 32768 | tf_op jit(solution)/shard_map/psum | solution.py:24
  (120 shorter events, 32.3 us)
Async XLA Ops:
  7.2 0.9 copy-start
  7.2 124.6 %all-reduce.11.cloned.1.call-start = ((), (), s32[]{:S(2)}) async-start(), calls=%async_computation | async-start | bytes 131072 | tf_op jit(solution)/shard_map/psum | solution.py:52
  14.7 1.9 copy-start.1
  16.6 4.5 copy-start.2
  21.1 381.5 %all-reduce.13.cloned.1.call-start = ((), (), s32[]{:S(2)}) async-start(), calls=%async_computation.1 | async-start | bytes 131072 | tf_op jit(solution)/shard_map/psum | solution.py:52
  277.6 395.5 %all-reduce.15.cloned.1.call-start = ((), (), s32[]{:S(2)}) async-start(), calls=%async_computation.2 | async-start | bytes 131072 | tf_op jit(solution)/shard_map/psum | solution.py:52
  548.1 395.6 %all-reduce.17.cloned.1.call-start = ((), (), s32[]{:S(2)}) async-start(), calls=%async_computation.3 | async-start | bytes 131072 | tf_op jit(solution)/shard_map/psum | solution.py:52
  818.6 395.5 %all-reduce.19.cloned.1.call-start = ((), (), s32[]{:S(2)}) async-start(), calls=%async_computation.4 | async-start | bytes 131072 | tf_op jit(solution)/shard_map/psum | solution.py:52
Sparse Core Ops, SparseCore 0:
  21.2 110.5 all-reduce.10
  277.7 124.8 all-reduce.12
  548.2 124.8 all-reduce.14
  818.8 124.8 all-reduce.16
  1089.3 124.8 all-reduce.18
where the time goes:
time: 1440 us; the launch traced here: 1430 us
  blocking collectives  982 us (68%)
  waiting for transfers between devices  219 us (15%)
  other arithmetic  122 us (8%)
  matrix products  85.4 us (6%)
  between operations  14.6 us (1%)
    psum x5, blocking collectives, body(): target_sum, compound_gram = lax.psum((second, gram_of(compound_raw)), 'cmp')  582 us
    psum x6, blocking collectives, target_total(): return lax.psum(partial_gram, 'tgt')  400 us
    psum x5, waiting for transfers between devices, body(): summed = lax.psum(first, 'tgt')  219 us
    another operation x30, other arithmetic, solve_normal(): lower = jnp.linalg.cholesky(normal)  65.2 us
    another operation x20, other arithmetic, solve_normal(): lax.linalg.triangular_solve(lower, middle, left_side=False, lower=True, t...  55.5 us
    dot_general x5, matrix products, body(): jnp.einsum('ijr,ir->jr', inner_again, compound_raw, precision=lax.Precisi...  38.5 us
    dot_general x5, matrix products, body(): jnp.einsum('ijr,jr->ir', inner, target_raw, precision=lax.Precision.HIGHEST)  29.6 us
  transfers between devices with their start and end apart: 5, of which 5 were waited for; matrix products, arithmetic and copies ran while one was open for 4% of the time, Pallas kernels for 0%

commit v1 on v0

--- a/solution.py
+++ b/solution.py
@@ -49,7 +49,7 @@
     for sweep in range(ITERS):
         inner = fetch()
         first = jnp.einsum("ijr,jr->ir", inner, target_raw, precision=lax.Precision.HIGHEST)
-        summed = lax.psum(first, "tgt")
+        summed = jnp.sum(lax.all_gather(first, "tgt"), axis=0)
         compound_raw = solve_normal(summed, target_gram * cond_gram)
         inner_again = fetch()
         second = jnp.einsum(

time: 1440 us -> 1220 us (0.85)
  waiting for transfers between devices: 219 us -> 0.22 us
    psum x5 -> x0, waiting for transfers between devices: 219 us -> none  [body(): summed = lax.psum(first, 'tgt')]
    psum x5, blocking collectives: 582 us -> 561 us  [body(): target_sum, compound_gram = lax.psum((second, gram_of(compound_raw)), 'cmp')]
    psum x6, blocking collectives: 400 us -> 419 us  [target_total(): return lax.psum(partial_gram, 'tgt')]
  transfers between devices with their start and end apart: 5 -> 5, of which waited for: 5 -> 0; matrix products, arithmetic and copies ran while one was open for 4% -> 5% of each run, Pallas kernels for 0% -> 0%
where the time goes in v1:
time: 1220 us
  blocking collectives  980 us (80%)
  other arithmetic  122 us (10%)
  matrix products  81.2 us (7%)
  local copies, waits for them, and re-layouts  16.7 us (1%)
  between operations  14.9 us (1%)
    psum x5, blocking collectives, body(): target_sum, compound_gram = lax.psum((second, gram_of(compound_raw)), 'cmp')  561 us
    psum x6, blocking collectives, target_total(): return lax.psum(partial_gram, 'tgt')  419 us
    another operation x30, other arithmetic, solve_normal(): lower = jnp.linalg.cholesky(normal)  65.2 us
    another operation x20, other arithmetic, solve_normal(): lax.linalg.triangular_solve(lower, middle, left_side=False, lower=True, t...  55.5 us
    dot_general x5, matrix products, body(): jnp.einsum('ijr,ir->jr', inner_again, compound_raw, precision=lax.Precisi...  38.5 us
    dot_general x5, matrix products, body(): jnp.einsum('ijr,jr->ir', inner, target_raw, precision=lax.Precision.HIGHEST)  29.6 us
  transfers between devices with their start and end apart: 5, of which 0 were waited for; matrix products, arithmetic and copies ran while one was open for 5% of the time, Pallas kernels for 0%

profile of v1, /device:TPU:1, one launch (start us, length us, event | category | flops | bytes accessed | tf_op | source)
XLA Modules:
  0.0 1215.9 jit_solution(17848104395204399373)
XLA Ops:
  8.1 6.6 fusion
  14.7 1.9 copy-done.1
  16.6 3.8 fusion.20
  21.3 50.2 %psum.112 = f32[64,64]{0,1:T(8,128)S(1)} all-reduce(f32[64,64]{0,1:T(8,128)S(1)} %fusion.112), channel_id=1, replica_groups=mesh['cmp'=32,'tgt'=16] {'tgt'}, use_global_device_ids=true, to_apply=%region_0.0 | all-reduce | flops 4096 | bytes 32768 | tf_op jit(solution)/shard_map/psum | solution.py:24
  71.8 5.8 cholesky.164
  79.0 4.9 custom-call.35
  83.9 1.5 copy.133
  86.3 7.7 fusion.18
  94.0 118.6 %all-reduce.4 = (f32[64,64]{0,1:T(8,128)S(1)}, f32[64,64]{0,1:T(8,128)S(1)}) all-reduce(f32[64,64]{0,1:T(8,128)S(1)} %bitcast.333, f32[64,64]{0,1:T(8,128)S(1)} %fusion.30), channel_id=1, replica_groups=mesh['cmp'=32,'tgt'=16] {'cmp'}, use_global_device_ids=true, to_apply=%region_5.9 | all-reduce | flops 8192 | bytes 65536 | tf_op jit(solution)/shard_map/psum | solution.py:58
  212.7 5.8 cholesky.175
  219.9 4.9 custom-call.37
  225.2 6.4 fusion.16
  232.5 74.1 %psum.115 = f32[64,64]{0,1:T(8,128)S(1)} all-reduce(f32[64,64]{0,1:T(8,128)S(1)} %fusion.84), channel_id=1, replica_groups=mesh['cmp'=32,'tgt'=16] {'tgt'}, use_global_device_ids=true, to_apply=%region_6.12 | all-reduce | flops 4096 | bytes 32768 | tf_op jit(solution)/shard_map/psum | solution.py:24
  306.7 5.8 cholesky.186
  313.9 4.9 custom-call.39
  318.8 1.5 copy.134
  321.2 7.7 fusion.14
  328.9 110.7 %all-reduce.3 = (f32[64,64]{0,1:T(8,128)S(1)}, f32[64,64]{0,1:T(8,128)S(1)}) all-reduce(f32[64,64]{0,1:T(8,128)S(1)} %bitcast.334, f32[64,64]{0,1:T(8,128)S(1)} %fusion.28), channel_id=1, replica_groups=mesh['cmp'=32,'tgt'=16] {'cmp'}, use_global_device_ids=true, to_apply=%region_9.15 | all-reduce | flops 8192 | bytes 65536 | tf_op jit(solution)/shard_map/psum | solution.py:58
  439.7 5.8 cholesky.197
  446.9 4.9 custom-call.41
  452.2 6.4 fusion.12
  459.5 73.9 %psum.118 = f32[64,64]{0,1:T(8,128)S(1)} all-reduce(f32[64,64]{0,1:T(8,128)S(1)} %fusion.74), channel_id=1, replica_groups=mesh['cmp'=32,'tgt'=16] {'tgt'}, use_global_device_ids=true, to_apply=%region_10.16 | all-reduce | flops 4096 | bytes 32768 | tf_op jit(solution)/shard_map/psum | solution.py:24
  533.5 5.8 cholesky.208
  540.7 4.9 custom-call.43
  545.6 1.5 copy.135
  548.0 7.7 fusion.10
  555.7 110.6 %all-reduce.2 = (f32[64,64]{0,1:T(8,128)S(1)}, f32[64,64]{0,1:T(8,128)S(1)}) all-reduce(f32[64,64]{0,1:T(8,128)S(1)} %bitcast.335, f32[64,64]{0,1:T(8,128)S(1)} %fusion.26), channel_id=1, replica_groups=mesh['cmp'=32,'tgt'=16] {'cmp'}, use_global_device_ids=true, to_apply=%region_13.19 | all-reduce | flops 8192 | bytes 65536 | tf_op jit(solution)/shard_map/psum | solution.py:58
  666.4 5.8 cholesky.219
  673.6 4.9 custom-call.45
  678.9 6.4 fusion.8
  686.2 74.2 %psum.121 = f32[64,64]{0,1:T(8,128)S(1)} all-reduce(f32[64,64]{0,1:T(8,128)S(1)} %fusion.64), channel_id=1, replica_groups=mesh['cmp'=32,'tgt'=16] {'tgt'}, use_global_device_ids=true, to_apply=%region_14.20 | all-reduce | flops 4096 | bytes 32768 | tf_op jit(solution)/shard_map/psum | solution.py:24
  760.5 5.8 cholesky.230
  767.7 4.9 custom-call.47
  772.7 1.5 copy.136
  775.0 7.7 fusion.6
  782.7 110.5 %all-reduce.1 = (f32[64,64]{0,1:T(8,128)S(1)}, f32[64,64]{0,1:T(8,128)S(1)}) all-reduce(f32[64,64]{0,1:T(8,128)S(1)} %bitcast.336, f32[64,64]{0,1:T(8,128)S(1)} %fusion.24), channel_id=1, replica_groups=mesh['cmp'=32,'tgt'=16] {'cmp'}, use_global_device_ids=true, to_apply=%region_17.23 | all-reduce | flops 8192 | bytes 65536 | tf_op jit(solution)/shard_map/psum | solution.py:58
  893.3 5.8 cholesky.241
  900.5 4.9 custom-call.49
  905.8 6.5 fusion.4
  913.2 74.1 %psum.124 = f32[64,64]{0,1:T(8,128)S(1)} all-reduce(f32[64,64]{0,1:T(8,128)S(1)} %fusion.54), channel_id=1, replica_groups=mesh['cmp'=32,'tgt'=16] {'tgt'}, use_global_device_ids=true, to_apply=%region_18.24 | all-reduce | flops 4096 | bytes 32768 | tf_op jit(solution)/shard_map/psum | solution.py:24
  987.3 5.8 cholesky.252
  994.5 4.9 custom-call.51
  999.4 1.5 copy.137
  1001.8 7.7 fusion.2
  1009.5 110.4 %all-reduce = (f32[64,64]{0,1:T(8,128)S(1)}, f32[64,64]{0,1:T(8,128)S(1)}) all-reduce(f32[64,64]{0,1:T(8,128)S(1)} %fusion.22, f32[64,64]{0,1:T(8,128)S(1)} %bitcast.337), channel_id=1, replica_groups=mesh['cmp'=32,'tgt'=16] {'cmp'}, use_global_device_ids=true, to_apply=%region_20.26 | all-reduce | flops 8192 | bytes 65536 | tf_op jit(solution)/shard_map/psum | solution.py:58
  1121.5 5.8 cholesky.263
  1128.7 4.9 custom-call.53
  1134.3 73.0 %psum.127 = f32[64,64]{1,0:T(8,128)S(1)} all-reduce(f32[64,64]{1,0:T(8,128)S(1)} %fusion.113), channel_id=1, replica_groups=mesh['cmp'=32,'tgt'=16] {'tgt'}, use_global_device_ids=true, to_apply=%region_22.28 | all-reduce | flops 4096 | bytes 32768 | tf_op jit(solution)/shard_map/psum | solution.py:24
  (130 shorter events, 29.1 us)
Async XLA Ops:
  7.2 0.9 copy-start
  7.2 76.7 %all-gather.11.cloned.1.call-start = ((), (), s32[]{:S(2)}) async-start(), calls=%async_computation | async-start | bytes 1114112 | tf_op jit(solution)/shard_map/all_gather | solution.py:52
  14.6 1.9 copy-start.1
  16.6 4.5 copy-start.2
  21.1 297.7 %all-gather.13.cloned.1.call-start = ((), (), s32[]{:S(2)}) async-start(), calls=%async_computation.1 | async-start | bytes 1114112 | tf_op jit(solution)/shard_map/all_gather | solution.py:52
  232.3 313.3 %all-gather.15.cloned.1.call-start = ((), (), s32[]{:S(2)}) async-start(), calls=%async_computation.2 | async-start | bytes 1114112 | tf_op jit(solution)/shard_map/all_gather | solution.py:52
  459.3 313.4 %all-gather.17.cloned.1.call-start = ((), (), s32[]{:S(2)}) async-start(), calls=%async_computation.3 | async-start | bytes 1114112 | tf_op jit(solution)/shard_map/all_gather | solution.py:52
  686.0 313.4 %all-gather.19.cloned.1.call-start = ((), (), s32[]{:S(2)}) async-start(), calls=%async_computation.4 | async-start | bytes 1114112 | tf_op jit(solution)/shard_map/all_gather | solution.py:52
Sparse Core Ops, SparseCore 0:
  21.2 46.7 all-gather.10
  232.4 62.8 all-gather.12
  459.4 62.5 all-gather.14
  686.1 62.9 all-gather.16
  913.1 62.7 all-gather.18
